TPU v7x, 256 devices: a whole 4x4x8 slice. The times are simulated.
256 devices in a mesh: outer: 16 (over y, z_hi), inner: 16 (over x, z_lo, core).
Axes of the slice: x: 4, y: 4, z: 8 (z_hi: 4, z_lo: 2; z = z_hi * 2 + z_lo), core: 2. Of those that a mesh axis runs over, the one named last changes fastest.
Arguments:
- hidden: bfloat16 [32768, 1024], P(('outer', 'inner')), may hold values from -24 to 24
- x_act: bfloat16 [32768, 2048], P(('outer', 'inner')), may hold values from -6 to 6
- dt_step: float32 [32768, 32], P(('outer', 'inner')), may hold values from 0.0014915534 to 0.44, as said below
- log_decay: float32 [32768, 32], P(('outer', 'inner')), may hold values from -0.81 to -8.85009766e-07, as said below
- w_bc: bfloat16 [1024, 128], P(('outer', 'inner')), may hold values from -0.1875 to 0.1875
- grad_y: bfloat16 [32768, 2048], P(('outer', 'inner')), may hold values from -0.19921875 to 0.19921875
Outputs:
- grad_x: float32 [32768, 2048], P(('outer', 'inner'))
- grad_hidden: float32 [32768, 1024], P(('outer', 'inner'))
- grad_proj: float32 [1024, 128], P(('outer', 'inner'))
Inputs may be any that keep to these rules, and one draw needn't show every extreme that they name: `dt_step`: Positive; constant in scale within each head apart from a factor within e**-0.5 to e**0.5. `log_decay`: Negative.
All inputs are finite; a program needn't handle non-finite values.
Results may differ from a plain program's by a relative error of at most 0.0029.
Values may be sent and summed in bfloat16 or wider, within the bound.
A program may use at most 64 MiB of HBM per device.

v0:
```python
import math
import jax
import jax.numpy as jnp
from jax import lax
from jax.sharding import PartitionSpec as P

BLOCK = 128
HIGH = lax.Precision.HIGHEST


def shifted(value, axis, steps):
    count = lax.axis_size(axis)
    first, last = (max(0, -steps), min(count, count - steps))
    return lax.ppermute(value, axis, [(source, source + steps) for source in range(first, last)])


def block_step(carried, pieces):
    inputs, decays, b_rows, c_rows = pieces
    length = inputs.shape[0]
    running = jnp.cumsum(decays, axis=0)
    row_ids = lax.broadcasted_iota(jnp.int32, (length, length), 0)
    col_ids = lax.broadcasted_iota(jnp.int32, (length, length), 1)
    causal = row_ids >= col_ids
    spread = running.T[:, :, None] - running.T[:, None, :]
    segment = jnp.where(causal[None], jnp.exp(jnp.where(causal[None], spread, 0.0)), 0.0)
    scores = jnp.einsum("in,jn->ij", c_rows, b_rows, precision=HIGH)
    outputs = jnp.einsum("hij,jhp->ihp", segment * scores[None], inputs, precision=HIGH)
    outputs = outputs + jnp.exp(running)[:, :, None] * jnp.einsum(
        "in,hpn->ihp", c_rows, carried, precision=HIGH
    )
    final_sum = running[-1]
    weights = jnp.exp(final_sum[None, :] - running)
    updated = jnp.exp(final_sum)[:, None, None] * carried + jnp.einsum(
        "jhp,jn->hpn", inputs * weights[:, :, None], b_rows, precision=HIGH
    )
    return (updated, outputs)


def scan_block(inputs, decays, b_rows, c_rows, carried, length):
    count = inputs.shape[0] // length
    pieces = (
        inputs.reshape((count, length) + inputs.shape[1:]),
        decays.reshape((count, length, decays.shape[1])),
        b_rows.reshape((count, length, b_rows.shape[1])),
        c_rows.reshape((count, length, c_rows.shape[1])),
    )
    final_state, outputs = lax.scan(block_step, carried, pieces)
    return (outputs.reshape(inputs.shape), final_state)


def combine(earlier, later):
    return (earlier[0] + later[0], jnp.exp(later[0])[:, None, None] * earlier[1] + later[1])


def doubling_prefix(own, backward):
    device_count = lax.axis_size(("outer", "inner"))
    distances = [1]
    reach = 1
    while reach < device_count:
        distances.append(reach)
        reach = reach * 2
    gathered = own
    for number, distance in enumerate(distances):
        if backward:
            arrived = shifted((gathered[0], gathered[1]), ("outer", "inner"), -distance)
        else:
            arrived = shifted((gathered[0], gathered[1]), ("outer", "inner"), distance)
        if number == 0:
            gathered = arrived
        else:
            gathered = combine(arrived, gathered)
    return gathered


def per_device(hidden, x_act, dt_step, log_decay, w_bc, grad_y):
    weights_full = lax.all_gather(w_bc, ("outer", "inner"), axis=0, tiled=True)
    state_width = weights_full.shape[1] // 2
    row_count = hidden.shape[0]
    head_count = dt_step.shape[1]
    head_size = x_act.shape[1] // head_count
    projected = jnp.dot(hidden, weights_full, preferred_element_type=jnp.float32)
    b_rows = projected[:, :state_width]
    c_rows = projected[:, state_width:]
    inputs = dt_step[:, :, None] * x_act.astype(jnp.float32).reshape(
        row_count, head_count, head_size
    )
    cotangent = grad_y.astype(jnp.float32).reshape(row_count, head_count, head_size)
    running = jnp.cumsum(log_decay, axis=0)
    totals = running[-1]
    own_state = jnp.einsum(
        "jhp,jn->hpn",
        inputs * jnp.exp(totals[None, :] - running)[:, :, None],
        b_rows,
        precision=HIGH,
    )
    own_adjoint = jnp.einsum(
        "ihp,in->hpn", cotangent * jnp.exp(running)[:, :, None], c_rows, precision=HIGH
    )
    state_in = doubling_prefix((totals, own_state), False)[1]
    adjoint_out = doubling_prefix((totals, own_adjoint), True)[1]

    def forward(inputs, b_rows, c_rows):
        return scan_block(inputs, log_decay, b_rows, c_rows, state_in, BLOCK)

    outputs, pullback = jax.vjp(forward, inputs, b_rows, c_rows)
    d_in, d_b, d_c = pullback((cotangent, adjoint_out))
    grad_x = (dt_step[:, :, None] * d_in).reshape(row_count, head_count * head_size)
    d_proj = jnp.concatenate([d_b, d_c], axis=1)
    d_low = d_proj.astype(jnp.bfloat16)
    grad_hidden = lax.dot_general(
        d_low, weights_full, (((1,), (1,)), ((), ())), preferred_element_type=jnp.float32
    )
    scale = 1.0 / math.sqrt(row_count * lax.axis_size("outer") * lax.axis_size("inner"))
    grad_proj = lax.psum_scatter(
        lax.dot_general(hidden, d_low, (((0,), (0,)), ((), ())), preferred_element_type=jnp.float32)
        * scale,
        ("outer", "inner"),
        scatter_dimension=0,
        tiled=True,
    )
    return (grad_x, grad_hidden, grad_proj)


def solution(mesh):
    in_specs = (
        P(("outer", "inner"), None),
        P(("outer", "inner"), None),
        P(("outer", "inner"), None),
        P(("outer", "inner"), None),
        P(("outer", "inner"), None),
        P(("outer", "inner"), None),
    )
    out_specs = (
        P(("outer", "inner"), None),
        P(("outer", "inner"), None),
        P(("outer", "inner"), None),
    )
    return jax.shard_map(
        per_device, mesh=mesh, in_specs=in_specs, out_specs=out_specs, check_vma=False
    )
```

profile of v0, /device:TPU:2, one launch (start us, length us, event | category | flops | bytes accessed | tf_op | source)
XLA Modules:
  0.0 1107.1 jit_solution(5641933597297097670)
XLA Ops:
  8.3 3.2 collective-permute-start
  11.5 1.9 collective-permute-start.17
  13.6 343.6 %all-gather = bf16[256,4,128]{2,1,0:T(4,128)(2,1)S(1)} all-gather(bf16[1,4,128]{2,1,0:T(4,128)(2,1)} %bitcast.65), channel_id=1, replica_groups=mesh['outer'=16,'inner'=16] {'outer','inner'}, dimensions={0}, use_global_device_ids=true | all-gather | bytes 263168 | tf_op jit(solution)/shard_map/all_gather | solution.py:76
  357.7 2.0 fusion.19
  359.7 3.2 collective-permute-start.8
  363.1 2.0 fusion.22
  365.1 1.9 collective-permute-start.25
  367.1 2.5 fusion
  370.6 1.0 bitcast_multiply_fusion.1
  371.9 3.5 fusion.3
  375.4 4.5 collective-permute-start.1
  380.0 1.9 collective-permute-start.18
  382.2 12.4 %collective-permute-start.2 = (f32[32]{0:T(128)S(1)}, f32[32]{0:T(128)S(1)}, u32[]{:S(2)}, u32[]{:S(2)}) collective-permute-start(f32[32]{0:T(128)S(1)} %get-tuple-element.192), channel_id=1, source_target_pairs={{2,0},{3,1},{4,2},{5,3},{6,4},{7,5},{8,6},{9,7},{10,8},{11,9},{12,... | collective-permute-start | bytes 392 | tf_op jit(solution)/shard_map/ppermute | solution.py:14
  394.6 1.9 collective-permute-start.19
  396.6 2.5 collective-permute-start.3
  399.1 1.9 collective-permute-done.19
  401.0 1.9 collective-permute-start.20
  402.9 2.5 collective-permute-start.9
  405.5 1.3 collective-permute-start.4
  406.8 6.1 collective-permute-start.21
  412.9 1.9 collective-permute-start.26
  414.8 1.3 collective-permute-start.5
  416.1 4.0 collective-permute-done.9
  420.1 1.4 multiply_add_fusion.14
  421.6 3.3 collective-permute-start.10
  424.8 11.8 %collective-permute-done.26 = f32[32,64,64]{2,1,0:T(8,128)S(1)} collective-permute-done((f32[32,64,64]{2,1,0:T(8,128)S(1)}, f32[32,64,64]{2,1,0:T(8,128)S(1)}, u32[]{:S(2)}, u32[]{:S(2)}) %collective-permute-start.26) | collective-permute-done | bytes 524320 | tf_op jit(solution)/shard_map/ppermute | solution.py:14
  436.8 1.9 collective-permute-start.27
  438.8 1.3 collective-permute-start.22
  440.1 9.5 collective-permute-done.10
  449.7 1.9 collective-permute-start.11
  451.7 42.2 %collective-permute-done.27 = f32[32,64,64]{2,1,0:T(8,128)S(1)} collective-permute-done((f32[32,64,64]{2,1,0:T(8,128)S(1)}, f32[32,64,64]{2,1,0:T(8,128)S(1)}, u32[]{:S(2)}, u32[]{:S(2)}) %collective-permute-start.27) | collective-permute-done | bytes 524320 | tf_op jit(solution)/shard_map/ppermute | solution.py:14
  494.0 1.9 collective-permute-start.28
  496.0 1.3 collective-permute-start.6
  497.4 1.3 collective-permute-start.12
  498.7 22.1 %collective-permute-done.28 = f32[32,64,64]{2,1,0:T(8,128)S(1)} collective-permute-done((f32[32,64,64]{2,1,0:T(8,128)S(1)}, f32[32,64,64]{2,1,0:T(8,128)S(1)}, u32[]{:S(2)}, u32[]{:S(2)}) %collective-permute-start.28) | collective-permute-done | bytes 524320 | tf_op jit(solution)/shard_map/ppermute | solution.py:14
  521.0 20.4 %collective-permute-start.29 = (f32[32,64,64]{2,1,0:T(8,128)S(1)}, f32[32,64,64]{2,1,0:T(8,128)S(1)}, u32[]{:S(2)}, u32[]{:S(2)}) collective-permute-start(f32[32,64,64]{2,1,0:T(8,128)S(1)} %multiply_add_fusion.4), channel_id=1, source_target_pairs={{0,8},{1,9},{2,10},{3,11},{4,12},{5,13},{6,14},{7,15},{8,16},{9,17... | collective-permute-start | bytes 1572872 | tf_op jit(solution)/shard_map/ppermute | solution.py:14
  541.5 1.3 collective-permute-start.23
  542.8 2.6 collective-permute-done.12
  545.5 1.5 collective-permute-start.13
  547.0 17.3 %collective-permute-done.29 = f32[32,64,64]{2,1,0:T(8,128)S(1)} collective-permute-done((f32[32,64,64]{2,1,0:T(8,128)S(1)}, f32[32,64,64]{2,1,0:T(8,128)S(1)}, u32[]{:S(2)}, u32[]{:S(2)}) %collective-permute-start.29) | collective-permute-done | bytes 524320 | tf_op jit(solution)/shard_map/ppermute | solution.py:14
  564.4 41.7 %collective-permute-start.30 = (f32[32,64,64]{2,1,0:T(8,128)S(1)}, f32[32,64,64]{2,1,0:T(8,128)S(1)}, u32[]{:S(2)}, u32[]{:S(2)}) collective-permute-start(f32[32,64,64]{2,1,0:T(8,128)S(1)} %multiply_add_fusion.3), channel_id=1, source_target_pairs={{0,16},{1,17},{2,18},{3,19},{4,20},{5,21},{6,22},{7,23},{8,24},{9,... | collective-permute-start | bytes 1572872 | tf_op jit(solution)/shard_map/ppermute | solution.py:14
  606.1 1.3 collective-permute-start.7
  607.4 6.8 collective-permute-done.13
  614.4 1.3 collective-permute-start.14
  615.7 20.4 %collective-permute-done.30 = f32[32,64,64]{2,1,0:T(8,128)S(1)} collective-permute-done((f32[32,64,64]{2,1,0:T(8,128)S(1)}, f32[32,64,64]{2,1,0:T(8,128)S(1)}, u32[]{:S(2)}, u32[]{:S(2)}) %collective-permute-start.30) | collective-permute-done | bytes 524320 | tf_op jit(solution)/shard_map/ppermute | solution.py:14
  636.3 1.4 collective-permute-start.31
  637.7 1.3 collective-permute-start.24
  639.0 9.2 collective-permute-done.14
  648.4 1.3 collective-permute-start.15
  649.7 11.0 collective-permute-done.31
  660.8 45.0 %collective-permute-start.32 = (f32[32,64,64]{2,1,0:T(8,128)S(1)}, f32[32,64,64]{2,1,0:T(8,128)S(1)}, u32[]{:S(2)}, u32[]{:S(2)}) collective-permute-start(f32[32,64,64]{2,1,0:T(8,128)S(1)} %multiply_add_fusion.1), channel_id=1, source_target_pairs={{0,64},{1,65},{2,66},{3,67},{4,68},{5,69},{6,70},{7,71},{8,72},{9,... | collective-permute-start | bytes 1572872 | tf_op jit(solution)/shard_map/ppermute | solution.py:14
  705.9 2.1 collective-permute-done.15
  708.1 1.3 collective-permute-start.16
  709.4 17.3 %collective-permute-done.32 = f32[32,64,64]{2,1,0:T(8,128)S(1)} collective-permute-done((f32[32,64,64]{2,1,0:T(8,128)S(1)}, f32[32,64,64]{2,1,0:T(8,128)S(1)}, u32[]{:S(2)}, u32[]{:S(2)}) %collective-permute-start.32) | collective-permute-done | bytes 524320 | tf_op jit(solution)/shard_map/ppermute | solution.py:14
  726.9 9.0 collective-permute-start.33
  735.9 18.5 %collective-permute-done.16 = f32[32,64,64]{2,1,0:T(8,128)S(1)} collective-permute-done((f32[32,64,64]{2,1,0:T(8,128)S(1)}, f32[32,64,64]{2,1,0:T(8,128)S(1)}, u32[]{:S(2)}, u32[]{:S(2)}) %collective-permute-start.16) | collective-permute-done | bytes 524320 | tf_op jit(solution)/shard_map/ppermute | solution.py:14
  754.4 2.0 fusion.11
  756.6 2.0 fusion.12
  758.6 1.0 fusion.8
  759.7 2.3 fusion.7
  762.0 1.3 copy.49
  763.3 1.0 fusion.48
  764.3 334.4 %all-reduce.3.cloned.1.call-done = f32[1024,128]{0,1:T(8,128)} async-done(((f32[1024,128]{0,1:T(8,128)}), f32[1024,128]{0,1:T(8,128)}) %all-reduce.3.cloned.1.call-update) | async-done | bytes 524304
  1098.7 0.9 constant_dynamic-slice_fusion
  (83 shorter events, 6.9 us)
Async XLA Ops:
  7.2 350.2 %copy-start = (bf16[128,1024]{1,0:T(8,128)(2,1)S(1)}, bf16[128,1024]{1,0:T(8,128)(2,1)}, u32[]{:S(2)}) copy-start(bf16[128,1024]{1,0:T(8,128)(2,1)} %param.6) | copy-start | bytes 786436
  7.2 349.9 %copy-start.5 = (bf16[128,2048]{1,0:T(8,128)(2,1)S(1)}, bf16[128,2048]{1,0:T(8,128)(2,1)}, u32[]{:S(2)}) copy-start(bf16[128,2048]{1,0:T(8,128)(2,1)} %param.11) | copy-start | bytes 1572868
  7.2 1091.5 %all-reduce.3.cloned.1.call-start = ((), (), s32[]{:S(2)}) async-start(), calls=%async_computation | async-start | bytes 1048576
  8.3 367.1 %collective-permute-start = (f32[32]{0:T(128)S(1)}, f32[32]{0:T(128)S(1)}, u32[]{:S(2)}, u32[]{:S(2)}) collective-permute-start(f32[32]{0:T(128)S(1)} %slice_bitcast_fusion), channel_id=1, source_target_pairs={{1,0},{2,1},{3,2},{4,3},{5,4},{6,5},{7,6},{8,7},{9,8},{10,9},{11,1... | collective-permute-start | bytes 392 | tf_op jit(solution)/shard_map/ppermute | solution.py:14
  11.5 368.4 %collective-permute-start.17 = (f32[32]{0:T(128)S(1)}, f32[32]{0:T(128)S(1)}, u32[]{:S(2)}, u32[]{:S(2)}) collective-permute-start(f32[32]{0:T(128)S(1)} %slice_bitcast_fusion), channel_id=1, source_target_pairs={{0,1},{1,2},{2,3},{3,4},{4,5},{5,6},{6,7},{7,8},{8,9},{9,10},{10,1... | collective-permute-start | bytes 392 | tf_op jit(solution)/shard_map/ppermute | solution.py:14
  357.1 2.5 copy-start.2
  357.4 5.4 copy-start.4
  359.7 3.4 copy-start.6
  359.7 43.2 %collective-permute-start.8 = (f32[32,64,64]{2,1,0:T(8,128)}, f32[32,64,64]{2,1,0:T(8,128)}, u32[]{:S(2)}, u32[]{:S(2)}) collective-permute-start(f32[32,64,64]{2,1,0:T(8,128)} %fusion.19), channel_id=1, source_target_pairs={{1,0},{2,1},{3,2},{4,3},{5,4},{6,5},{7,6},{8,7},{9,8},{10,9},{11,1... | collective-permute-start | bytes 1572872 | tf_op jit(solution)/shard_map/ppermute | solution.py:14
  365.1 47.8 %collective-permute-start.25 = (f32[32,64,64]{2,1,0:T(8,128)}, f32[32,64,64]{2,1,0:T(8,128)S(1)}, u32[]{:S(2)}, u32[]{:S(2)}) collective-permute-start(f32[32,64,64]{2,1,0:T(8,128)} %fusion.22), channel_id=1, source_target_pairs={{0,1},{1,2},{2,3},{3,4},{4,5},{5,6},{6,7},{7,8},{8,9},{9,10},{10,1... | collective-permute-start | bytes 1572872 | tf_op jit(solution)/shard_map/ppermute | solution.py:14
  375.4 6.8 collective-permute-start.1
  380.0 14.6 %collective-permute-start.18 = (f32[32]{0:T(128)S(1)}, f32[32]{0:T(128)S(1)}, u32[]{:S(2)}, u32[]{:S(2)}) collective-permute-start(f32[32]{0:T(128)S(1)} %collective-permute-done.17), channel_id=1, source_target_pairs={{0,1},{1,2},{2,3},{3,4},{4,5},{5,6},{6,7},{7,8},{8,9},{9,10},{10,1... | collective-permute-start | bytes 392 | tf_op jit(solution)/shard_map/ppermute | solution.py:14
  382.2 14.3 %collective-permute-start.2 = (f32[32]{0:T(128)S(1)}, f32[32]{0:T(128)S(1)}, u32[]{:S(2)}, u32[]{:S(2)}) collective-permute-start(f32[32]{0:T(128)S(1)} %get-tuple-element.192), channel_id=1, source_target_pairs={{2,0},{3,1},{4,2},{5,3},{6,4},{7,5},{8,6},{9,7},{10,8},{11,9},{12,... | collective-permute-start | bytes 392 | tf_op jit(solution)/shard_map/ppermute | solution.py:14
  394.6 6.3 collective-permute-start.19
  396.6 8.9 collective-permute-start.3
  401.0 5.8 collective-permute-start.20
  402.9 17.2 %collective-permute-start.9 = (f32[32,64,64]{2,1,0:T(8,128)}, f32[32,64,64]{2,1,0:T(8,128)S(1)}, u32[]{:S(2)}, u32[]{:S(2)}) collective-permute-start(f32[32,64,64]{2,1,0:T(8,128)} %collective-permute-done.8), channel_id=1, source_target_pairs={{1,0},{2,1},{3,2},{4,3},{5,4},{6,5},{7,6},{8,7},{9,8},{10,9},{11,1... | collective-permute-start | bytes 1572872 | tf_op jit(solution)/shard_map/ppermute | solution.py:14
  405.5 9.3 collective-permute-start.4
  406.8 32.0 %collective-permute-start.21 = (f32[32]{0:T(128)S(1)}, f32[32]{0:T(128)S(1)}, u32[]{:S(2)}, u32[]{:S(2)}) collective-permute-start(f32[32]{0:T(128)S(1)} %get-tuple-element.176), channel_id=1, source_target_pairs={{0,8},{1,9},{2,10},{3,11},{4,12},{5,13},{6,14},{7,15},{8,16},{9,17... | collective-permute-start | bytes 392 | tf_op jit(solution)/shard_map/ppermute | solution.py:14
  412.9 23.8 %collective-permute-start.26 = (f32[32,64,64]{2,1,0:T(8,128)S(1)}, f32[32,64,64]{2,1,0:T(8,128)S(1)}, u32[]{:S(2)}, u32[]{:S(2)}) collective-permute-start(f32[32,64,64]{2,1,0:T(8,128)S(1)} %collective-permute-done.25), channel_id=1, source_target_pairs={{0,1},{1,2},{2,3},{3,4},{4,5},{5,6},{6,7},{7,8},{8,9},{9,10},{10,1... | collective-permute-start | bytes 1572872 | tf_op jit(solution)/shard_map/ppermute | solution.py:14
  414.8 81.1 %collective-permute-start.5 = (f32[32]{0:T(128)S(1)}, f32[32]{0:T(128)S(1)}, u32[]{:S(2)}, u32[]{:S(2)}) collective-permute-start(f32[32]{0:T(128)S(1)} %get-tuple-element.186), channel_id=1, source_target_pairs={{16,0},{17,1},{18,2},{19,3},{20,4},{21,5},{22,6},{23,7},{24,8},{25... | collective-permute-start | bytes 392 | tf_op jit(solution)/shard_map/ppermute | solution.py:14
  421.6 28.0 %collective-permute-start.10 = (f32[32,64,64]{2,1,0:T(8,128)S(1)}, f32[32,64,64]{2,1,0:T(8,128)S(1)}, u32[]{:S(2)}, u32[]{:S(2)}) collective-permute-start(f32[32,64,64]{2,1,0:T(8,128)S(1)} %multiply_add_fusion.14), channel_id=1, source_target_pairs={{2,0},{3,1},{4,2},{5,3},{6,4},{7,5},{8,6},{9,7},{10,8},{11,9},{12,... | collective-permute-start | bytes 1572872 | tf_op jit(solution)/shard_map/ppermute | solution.py:14
  436.8 57.0 %collective-permute-start.27 = (f32[32,64,64]{2,1,0:T(8,128)S(1)}, f32[32,64,64]{2,1,0:T(8,128)S(1)}, u32[]{:S(2)}, u32[]{:S(2)}) collective-permute-start(f32[32,64,64]{2,1,0:T(8,128)S(1)} %multiply_add_fusion.6), channel_id=1, source_target_pairs={{0,2},{1,3},{2,4},{3,5},{4,6},{5,7},{6,8},{7,9},{8,10},{9,11},{10,... | collective-permute-start | bytes 1572872 | tf_op jit(solution)/shard_map/ppermute | solution.py:14
  438.8 102.7 %collective-permute-start.22 = (f32[32]{0:T(128)S(1)}, f32[32]{0:T(128)S(1)}, u32[]{:S(2)}, u32[]{:S(2)}) collective-permute-start(f32[32]{0:T(128)S(1)} %get-tuple-element.174), channel_id=1, source_target_pairs={{0,16},{1,17},{2,18},{3,19},{4,20},{5,21},{6,22},{7,23},{8,24},{9,... | collective-permute-start | bytes 392 | tf_op jit(solution)/shard_map/ppermute | solution.py:14
  449.7 47.5 %collective-permute-start.11 = (f32[32,64,64]{2,1,0:T(8,128)S(1)}, f32[32,64,64]{2,1,0:T(8,128)S(1)}, u32[]{:S(2)}, u32[]{:S(2)}) collective-permute-start(f32[32,64,64]{2,1,0:T(8,128)S(1)} %multiply_add_fusion.13), channel_id=1, source_target_pairs={{4,0},{5,1},{6,2},{7,3},{8,4},{9,5},{10,6},{11,7},{12,8},{13,9},{1... | collective-permute-start | bytes 1572872 | tf_op jit(solution)/shard_map/ppermute | solution.py:14
  494.0 26.8 %collective-permute-start.28 = (f32[32,64,64]{2,1,0:T(8,128)S(1)}, f32[32,64,64]{2,1,0:T(8,128)S(1)}, u32[]{:S(2)}, u32[]{:S(2)}) collective-permute-start(f32[32,64,64]{2,1,0:T(8,128)S(1)} %multiply_add_fusion.5), channel_id=1, source_target_pairs={{0,4},{1,5},{2,6},{3,7},{4,8},{5,9},{6,10},{7,11},{8,12},{9,13},{1... | collective-permute-start | bytes 1572872 | tf_op jit(solution)/shard_map/ppermute | solution.py:14
  496.0 110.1 %collective-permute-start.6 = (f32[32]{0:T(128)S(1)}, f32[32]{0:T(128)S(1)}, u32[]{:S(2)}, u32[]{:S(2)}) collective-permute-start(f32[32]{0:T(128)S(1)} %get-tuple-element.184), channel_id=1, source_target_pairs={{32,0},{33,1},{34,2},{35,3},{36,4},{37,5},{38,6},{39,7},{40,8},{41... | collective-permute-start | bytes 392 | tf_op jit(solution)/shard_map/ppermute | solution.py:14
  497.4 47.9 %collective-permute-start.12 = (f32[32,64,64]{2,1,0:T(8,128)S(1)}, f32[32,64,64]{2,1,0:T(8,128)S(1)}, u32[]{:S(2)}, u32[]{:S(2)}) collective-permute-start(f32[32,64,64]{2,1,0:T(8,128)S(1)} %multiply_add_fusion.12), channel_id=1, source_target_pairs={{8,0},{9,1},{10,2},{11,3},{12,4},{13,5},{14,6},{15,7},{16,8},{17,9... | collective-permute-start | bytes 1572872 | tf_op jit(solution)/shard_map/ppermute | solution.py:14
  521.0 43.3 %collective-permute-start.29 = (f32[32,64,64]{2,1,0:T(8,128)S(1)}, f32[32,64,64]{2,1,0:T(8,128)S(1)}, u32[]{:S(2)}, u32[]{:S(2)}) collective-permute-start(f32[32,64,64]{2,1,0:T(8,128)S(1)} %multiply_add_fusion.4), channel_id=1, source_target_pairs={{0,8},{1,9},{2,10},{3,11},{4,12},{5,13},{6,14},{7,15},{8,16},{9,17... | collective-permute-start | bytes 1572872 | tf_op jit(solution)/shard_map/ppermute | solution.py:14
  541.5 96.2 %collective-permute-start.23 = (f32[32]{0:T(128)S(1)}, f32[32]{0:T(128)S(1)}, u32[]{:S(2)}, u32[]{:S(2)}) collective-permute-start(f32[32]{0:T(128)S(1)} %get-tuple-element.172), channel_id=1, source_target_pairs={{0,32},{1,33},{2,34},{3,35},{4,36},{5,37},{6,38},{7,39},{8,40},{9,... | collective-permute-start | bytes 392 | tf_op jit(solution)/shard_map/ppermute | solution.py:14
  545.5 68.8 %collective-permute-start.13 = (f32[32,64,64]{2,1,0:T(8,128)S(1)}, f32[32,64,64]{2,1,0:T(8,128)S(1)}, u32[]{:S(2)}, u32[]{:S(2)}) collective-permute-start(f32[32,64,64]{2,1,0:T(8,128)S(1)} %multiply_add_fusion.11), channel_id=1, source_target_pairs={{16,0},{17,1},{18,2},{19,3},{20,4},{21,5},{22,6},{23,7},{24,8},{25... | collective-permute-start | bytes 1572872 | tf_op jit(solution)/shard_map/ppermute | solution.py:14
  564.4 71.6 %collective-permute-start.30 = (f32[32,64,64]{2,1,0:T(8,128)S(1)}, f32[32,64,64]{2,1,0:T(8,128)S(1)}, u32[]{:S(2)}, u32[]{:S(2)}) collective-permute-start(f32[32,64,64]{2,1,0:T(8,128)S(1)} %multiply_add_fusion.3), channel_id=1, source_target_pairs={{0,16},{1,17},{2,18},{3,19},{4,20},{5,21},{6,22},{7,23},{8,24},{9,... | collective-permute-start | bytes 1572872 | tf_op jit(solution)/shard_map/ppermute | solution.py:14
  606.1 99.7 %collective-permute-start.7 = (f32[32]{0:T(128)S(1)}, f32[32]{0:T(128)S(1)}, u32[]{:S(2)}, u32[]{:S(2)}) collective-permute-start(f32[32]{0:T(128)S(1)} %get-tuple-element.182), channel_id=1, source_target_pairs={{64,0},{65,1},{66,2},{67,3},{68,4},{69,5},{70,6},{71,7},{72,8},{73... | collective-permute-start | bytes 392 | tf_op jit(solution)/shard_map/ppermute | solution.py:14
  614.4 33.8 %collective-permute-start.14 = (f32[32,64,64]{2,1,0:T(8,128)S(1)}, f32[32,64,64]{2,1,0:T(8,128)S(1)}, u32[]{:S(2)}, u32[]{:S(2)}) collective-permute-start(f32[32,64,64]{2,1,0:T(8,128)S(1)} %multiply_add_fusion.10), channel_id=1, source_target_pairs={{32,0},{33,1},{34,2},{35,3},{36,4},{37,5},{38,6},{39,7},{40,8},{41... | collective-permute-start | bytes 1572872 | tf_op jit(solution)/shard_map/ppermute | solution.py:14
  636.3 24.4 %collective-permute-start.31 = (f32[32,64,64]{2,1,0:T(8,128)S(1)}, f32[32,64,64]{2,1,0:T(8,128)S(1)}, u32[]{:S(2)}, u32[]{:S(2)}) collective-permute-start(f32[32,64,64]{2,1,0:T(8,128)S(1)} %multiply_add_fusion.2), channel_id=1, source_target_pairs={{0,32},{1,33},{2,34},{3,35},{4,36},{5,37},{6,38},{7,39},{8,40},{9,... | collective-permute-start | bytes 1572872 | tf_op jit(solution)/shard_map/ppermute | solution.py:14
  637.7 98.2 %collective-permute-start.24 = (f32[32]{0:T(128)S(1)}, f32[32]{0:T(128)S(1)}, u32[]{:S(2)}, u32[]{:S(2)}) collective-permute-start(f32[32]{0:T(128)S(1)} %get-tuple-element.170), channel_id=1, source_target_pairs={{0,64},{1,65},{2,66},{3,67},{4,68},{5,69},{6,70},{7,71},{8,72},{9,... | collective-permute-start | bytes 392 | tf_op jit(solution)/shard_map/ppermute | solution.py:14
  648.4 59.6 %collective-permute-start.15 = (f32[32,64,64]{2,1,0:T(8,128)S(1)}, f32[32,64,64]{2,1,0:T(8,128)S(1)}, u32[]{:S(2)}, u32[]{:S(2)}) collective-permute-start(f32[32,64,64]{2,1,0:T(8,128)S(1)} %multiply_add_fusion.9), channel_id=1, source_target_pairs={{64,0},{65,1},{66,2},{67,3},{68,4},{69,5},{70,6},{71,7},{72,8},{73... | collective-permute-start | bytes 1572872 | tf_op jit(solution)/shard_map/ppermute | solution.py:14
  660.8 65.9 %collective-permute-start.32 = (f32[32,64,64]{2,1,0:T(8,128)S(1)}, f32[32,64,64]{2,1,0:T(8,128)S(1)}, u32[]{:S(2)}, u32[]{:S(2)}) collective-permute-start(f32[32,64,64]{2,1,0:T(8,128)S(1)} %multiply_add_fusion.1), channel_id=1, source_target_pairs={{0,64},{1,65},{2,66},{3,67},{4,68},{5,69},{6,70},{7,71},{8,72},{9,... | collective-permute-start | bytes 1572872 | tf_op jit(solution)/shard_map/ppermute | solution.py:14
  705.9 48.5 %copy-start.8 = (f32[32]{0:T(128)}, f32[32]{0:T(128)S(1)}, u32[]{:S(2)}) copy-start(f32[32]{0:T(128)S(1)} %add_exponential_fusion.1) | copy-start | bytes 388
  708.1 46.3 %collective-permute-start.16 = (f32[32,64,64]{2,1,0:T(8,128)S(1)}, f32[32,64,64]{2,1,0:T(8,128)S(1)}, u32[]{:S(2)}, u32[]{:S(2)}) collective-permute-start(f32[32,64,64]{2,1,0:T(8,128)S(1)} %multiply_add_fusion.8), channel_id=1, source_target_pairs={{128,0},{129,1},{130,2},{131,3},{132,4},{133,5},{134,6},{135,7},{1... | collective-permute-start | bytes 1572872 | tf_op jit(solution)/shard_map/ppermute | solution.py:14
  726.9 29.7 %collective-permute-start.33 = (f32[32,64,64]{2,1,0:T(8,128)S(1)}, f32[32,64,64]{2,1,0:T(8,128)S(1)}, u32[]{:S(2)}, u32[]{:S(2)}) collective-permute-start(f32[32,64,64]{2,1,0:T(8,128)S(1)} %multiply_add_fusion), channel_id=1, source_target_pairs={{0,128},{1,129},{2,130},{3,131},{4,132},{5,133},{6,134},{7,135},{8... | collective-permute-start | bytes 1572872 | tf_op jit(solution)/shard_map/ppermute | solution.py:14
  735.9 20.8 %copy-start.1 = (f32[128,2048]{0,1:T(8,128)S(1)}, f32[128,2048]{0,1:T(8,128)}, u32[]{:S(2)}) copy-start(f32[128,2048]{0,1:T(8,128)} %bitcast_multiply_fusion.1) | copy-start | bytes 3145732
  735.9 20.8 %copy-start.7 = (f32[128,64]{0,1:T(8,128)S(1)}, f32[128,64]{0,1:T(8,128)}, u32[]{:S(2)}) copy-start(f32[128,64]{0,1:T(8,128)} %fusion.44) | copy-start | bytes 98308
  758.6 1.1 copy-start.9
  762.0 1.3 copy-start.3
Sparse Core Ops, SparseCore 0:
  759.8 338.8 all-reduce.2
where the time goes:
time: 1110 us
  waiting for transfers between devices  532 us (48%)
  blocking collectives  344 us (31%)
  starting transfers between devices  188 us (17%)
  matrix products  19.8 us (2%)
  between operations  14.8 us (1%)
    all_gather x1, blocking collectives, per_device(): weights_full = lax.all_gather(w_bc, ('outer', 'inner'), axis=0, tiled=True)  344 us
    unnamed x2, waiting for transfers between devices  334 us
    ppermute x34, waiting for transfers between devices, shifted(): lax.ppermute(value, axis, [(source, source + steps) for source in range(f...  197 us
    ppermute x34, starting transfers between devices, shifted(): lax.ppermute(value, axis, [(source, source + steps) for source in range(f...  188 us
  transfers between devices with their start and end apart: 35, of which 18 were waited for; matrix products, arithmetic and copies ran while one was open for 2% of the time, Pallas kernels for 0%

commit v1 on v0

--- a/solution.py
+++ b/solution.py
@@ -73,7 +73,16 @@
 
 
 def per_device(hidden, x_act, dt_step, log_decay, w_bc, grad_y):
-    weights_full = lax.all_gather(w_bc, ("outer", "inner"), axis=0, tiled=True)
+    lead_group = lambda chunk: jnp.concatenate(
+        lax.all_to_all(
+            jnp.stack(lax.axis_size(("outer", "inner")) * [chunk]),
+            ("outer", "inner"),
+            split_axis=0,
+            concat_axis=0,
+        ),
+        0,
+    )
+    weights_full = lead_group(w_bc)
     state_width = weights_full.shape[1] // 2
     row_count = hidden.shape[0]
     head_count = dt_step.shape[1]

time: 1110 us -> 817 us (0.74)
  blocking collectives: 344 us -> 0 us
  starting transfers between devices: 188 us -> 242 us
    all_gather x1 -> x0, blocking collectives: 344 us -> none  [per_device(): weights_full = lax.all_gather(w_bc, ('outer', 'inner'), axis=0, tiled=True)]
    ppermute x34, starting transfers between devices: 188 us -> 225 us  [shifted(): lax.ppermute(value, axis, [(source, source + steps) for source in range(f...]
    all_to_all x0 -> x1, starting transfers between devices: none -> 17.2 us  [per_device(): lax.all_to_all(jnp.stack(lax.axis_size(('outer', 'inner')) * [chunk]), ('...]
    ppermute x34, waiting for transfers between devices: 197 us -> 209 us  [shifted(): lax.ppermute(value, axis, [(source, source + steps) for source in range(f...]
    unnamed x2, waiting for transfers between devices: 334 us -> 323 us
  transfers between devices with their start and end apart: 35 -> 36, of which waited for: 18 -> 17; matrix products, arithmetic and copies ran while one was open for 2% -> 3% of each run, Pallas kernels for 0% -> 0%
where the time goes in v1:
time: 817 us; the launch traced here: 815 us
  waiting for transfers between devices  532 us (65%)
  starting transfers between devices  242 us (30%)
  matrix products  17.2 us (2%)
  between operations  14.9 us (2%)
    unnamed x2, waiting for transfers between devices  323 us
    ppermute x34, starting transfers between devices, shifted(): lax.ppermute(value, axis, [(source, source + steps) for source in range(f...  225 us
    ppermute x34, waiting for transfers between devices, shifted(): lax.ppermute(value, axis, [(source, source + steps) for source in range(f...  209 us
    all_to_all x1, starting transfers between devices, per_device(): lax.all_to_all(jnp.stack(lax.axis_size(('outer', 'inner')) * [chunk]), ('...  17.2 us
  transfers between devices with their start and end apart: 36, of which 17 were waited for; matrix products, arithmetic and copies ran while one was open for 3% of the time, Pallas kernels for 0%

profile of v1, /device:TPU:2, one launch (start us, length us, event | category | flops | bytes accessed | tf_op | source)
XLA Modules:
  0.0 815.4 jit_solution(3887397964865568706)
XLA Ops:
  8.3 3.4 collective-permute-start
  11.6 1.9 collective-permute-start.17
  13.6 1.5 stack.2
  15.0 17.2 %all-to-all-start = ((bf16[256,4,128]{2,1,0:T(4,128)(2,1)}), bf16[256,4,128]{2,1,0:T(4,128)(2,1)S(1)}, u32[]{:S(2)}, u32[]{:S(2)}) async-start(bf16[256,4,128]{2,1,0:T(4,128)(2,1)} %stack.2), calls=%async_computation | async-start | bytes 524288 | tf_op jit(solution)/shard_map/all_to_all | solution.py:77
  33.0 1.1 bitcast_multiply_fusion.1
  34.1 2.4 fusion
  36.6 3.2 collective-permute-start.1
  39.8 1.9 collective-permute-start.18
  41.8 2.7 collective-permute-start.2
  44.5 1.1 collective-permute-done.18
  45.6 2.1 collective-permute-start.19
  47.7 3.2 collective-permute-start.3
  50.9 1.0 collective-permute-done.19
  51.9 3.4 collective-permute-start.20
  55.4 1.3 collective-permute-start.4
  57.4 8.5 %collective-permute-start.21 = (f32[32]{0:T(128)S(1)}, f32[32]{0:T(128)S(1)}, u32[]{:S(2)}, u32[]{:S(2)}) collective-permute-start(f32[32]{0:T(128)S(1)} %get-tuple-element.176), channel_id=1, source_target_pairs={{0,8},{1,9},{2,10},{3,11},{4,12},{5,13},{6,14},{7,15},{8,16},{9,17... | collective-permute-start | bytes 392 | tf_op jit(solution)/shard_map/ppermute | solution.py:14
  66.2 1.0 fusion.19
  67.1 1.9 collective-permute-start.8
  69.1 1.3 collective-permute-start.5
  70.4 1.0 fusion.22
  71.4 2.4 collective-permute-start.25
  73.8 9.1 %collective-permute-start.22 = (f32[32]{0:T(128)S(1)}, f32[32]{0:T(128)S(1)}, u32[]{:S(2)}, u32[]{:S(2)}) collective-permute-start(f32[32]{0:T(128)S(1)} %get-tuple-element.174), channel_id=1, source_target_pairs={{0,16},{1,17},{2,18},{3,19},{4,20},{5,21},{6,22},{7,23},{8,24},{9,... | collective-permute-start | bytes 392 | tf_op jit(solution)/shard_map/ppermute | solution.py:14
  82.9 4.0 collective-permute-done.8
  87.0 4.7 collective-permute-start.9
  91.7 1.3 collective-permute-start.6
  93.0 12.6 %collective-permute-start.23 = (f32[32]{0:T(128)S(1)}, f32[32]{0:T(128)S(1)}, u32[]{:S(2)}, u32[]{:S(2)}) collective-permute-start(f32[32]{0:T(128)S(1)} %get-tuple-element.172), channel_id=1, source_target_pairs={{0,32},{1,33},{2,34},{3,35},{4,36},{5,37},{6,38},{7,39},{8,40},{9,... | collective-permute-start | bytes 392 | tf_op jit(solution)/shard_map/ppermute | solution.py:14
  105.6 1.9 collective-permute-start.26
  107.5 7.2 collective-permute-done.6
  114.7 1.3 collective-permute-start.7
  116.2 3.2 collective-permute-start.10
  119.3 5.0 collective-permute-done.26
  124.5 1.9 collective-permute-start.27
  126.5 11.9 %collective-permute-start.24 = (f32[32]{0:T(128)S(1)}, f32[32]{0:T(128)S(1)}, u32[]{:S(2)}, u32[]{:S(2)}) collective-permute-start(f32[32]{0:T(128)S(1)} %get-tuple-element.170), channel_id=1, source_target_pairs={{0,64},{1,65},{2,66},{3,67},{4,68},{5,69},{6,70},{7,71},{8,72},{9,... | collective-permute-start | bytes 392 | tf_op jit(solution)/shard_map/ppermute | solution.py:14
  138.4 5.7 collective-permute-done.10
  144.3 1.9 collective-permute-start.11
  146.3 42.1 %collective-permute-done.27 = f32[32,64,64]{2,1,0:T(8,128)S(1)} collective-permute-done((f32[32,64,64]{2,1,0:T(8,128)S(1)}, f32[32,64,64]{2,1,0:T(8,128)S(1)}, u32[]{:S(2)}, u32[]{:S(2)}) %collective-permute-start.27) | collective-permute-done | bytes 524320 | tf_op jit(solution)/shard_map/ppermute | solution.py:14
  188.5 1.9 collective-permute-start.28
  190.7 1.3 collective-permute-start.12
  192.0 27.3 %collective-permute-done.28 = f32[32,64,64]{2,1,0:T(8,128)S(1)} collective-permute-done((f32[32,64,64]{2,1,0:T(8,128)S(1)}, f32[32,64,64]{2,1,0:T(8,128)S(1)}, u32[]{:S(2)}, u32[]{:S(2)}) %collective-permute-start.28) | collective-permute-done | bytes 524320 | tf_op jit(solution)/shard_map/ppermute | solution.py:14
  219.5 1.4 collective-permute-start.29
  221.1 1.3 collective-permute-start.13
  222.4 21.7 %collective-permute-done.29 = f32[32,64,64]{2,1,0:T(8,128)S(1)} collective-permute-done((f32[32,64,64]{2,1,0:T(8,128)S(1)}, f32[32,64,64]{2,1,0:T(8,128)S(1)}, u32[]{:S(2)}, u32[]{:S(2)}) %collective-permute-start.29) | collective-permute-done | bytes 524320 | tf_op jit(solution)/shard_map/ppermute | solution.py:14
  244.3 3.1 collective-permute-start.30
  247.8 1.3 collective-permute-start.14
  249.1 10.5 %collective-permute-done.30 = f32[32,64,64]{2,1,0:T(8,128)S(1)} collective-permute-done((f32[32,64,64]{2,1,0:T(8,128)S(1)}, f32[32,64,64]{2,1,0:T(8,128)S(1)}, u32[]{:S(2)}, u32[]{:S(2)}) %collective-permute-start.30) | collective-permute-done | bytes 524320 | tf_op jit(solution)/shard_map/ppermute | solution.py:14
  259.7 61.1 %collective-permute-start.31 = (f32[32,64,64]{2,1,0:T(8,128)S(1)}, f32[32,64,64]{2,1,0:T(8,128)S(1)}, u32[]{:S(2)}, u32[]{:S(2)}) collective-permute-start(f32[32,64,64]{2,1,0:T(8,128)S(1)} %multiply_add_fusion.2), channel_id=1, source_target_pairs={{0,32},{1,33},{2,34},{3,35},{4,36},{5,37},{6,38},{7,39},{8,40},{9,... | collective-permute-start | bytes 1572872 | tf_op jit(solution)/shard_map/ppermute | solution.py:14
  320.8 3.5 fusion.3
  324.3 10.6 %collective-permute-done.14 = f32[32,64,64]{2,1,0:T(8,128)S(1)} collective-permute-done((f32[32,64,64]{2,1,0:T(8,128)S(1)}, f32[32,64,64]{2,1,0:T(8,128)S(1)}, u32[]{:S(2)}, u32[]{:S(2)}) %collective-permute-start.14) | collective-permute-done | bytes 524320 | tf_op jit(solution)/shard_map/ppermute | solution.py:14
  335.1 1.3 collective-permute-start.15
  336.4 31.2 %collective-permute-done.31 = f32[32,64,64]{2,1,0:T(8,128)S(1)} collective-permute-done((f32[32,64,64]{2,1,0:T(8,128)S(1)}, f32[32,64,64]{2,1,0:T(8,128)S(1)}, u32[]{:S(2)}, u32[]{:S(2)}) %collective-permute-start.31) | collective-permute-done | bytes 524320 | tf_op jit(solution)/shard_map/ppermute | solution.py:14
  367.8 52.0 %collective-permute-start.32 = (f32[32,64,64]{2,1,0:T(8,128)S(1)}, f32[32,64,64]{2,1,0:T(8,128)S(1)}, u32[]{:S(2)}, u32[]{:S(2)}) collective-permute-start(f32[32,64,64]{2,1,0:T(8,128)S(1)} %multiply_add_fusion.1), channel_id=1, source_target_pairs={{0,64},{1,65},{2,66},{3,67},{4,68},{5,69},{6,70},{7,71},{8,72},{9,... | collective-permute-start | bytes 1572872 | tf_op jit(solution)/shard_map/ppermute | solution.py:14
  420.3 1.3 collective-permute-start.16
  421.6 21.1 %collective-permute-done.32 = f32[32,64,64]{2,1,0:T(8,128)S(1)} collective-permute-done((f32[32,64,64]{2,1,0:T(8,128)S(1)}, f32[32,64,64]{2,1,0:T(8,128)S(1)}, u32[]{:S(2)}, u32[]{:S(2)}) %collective-permute-start.32) | collective-permute-done | bytes 524320 | tf_op jit(solution)/shard_map/ppermute | solution.py:14
  442.8 11.7 %collective-permute-start.33 = (f32[32,64,64]{2,1,0:T(8,128)S(1)}, f32[32,64,64]{2,1,0:T(8,128)S(1)}, u32[]{:S(2)}, u32[]{:S(2)}) collective-permute-start(f32[32,64,64]{2,1,0:T(8,128)S(1)} %multiply_add_fusion), channel_id=1, source_target_pairs={{0,128},{1,129},{2,130},{3,131},{4,132},{5,133},{6,134},{7,135},{8... | collective-permute-start | bytes 1572872 | tf_op jit(solution)/shard_map/ppermute | solution.py:14
  454.7 18.4 %collective-permute-done.16 = f32[32,64,64]{2,1,0:T(8,128)S(1)} collective-permute-done((f32[32,64,64]{2,1,0:T(8,128)S(1)}, f32[32,64,64]{2,1,0:T(8,128)S(1)}, u32[]{:S(2)}, u32[]{:S(2)}) %collective-permute-start.16) | collective-permute-done | bytes 524320 | tf_op jit(solution)/shard_map/ppermute | solution.py:14
  473.1 2.0 fusion.11
  475.1 1.1 collective-permute-done.33
  476.2 2.0 fusion.12
  478.2 1.0 fusion.8
  479.3 2.3 fusion.7
  481.6 1.3 copy.49
  482.9 1.0 fusion.48
  483.9 323.1 %all-reduce.3.cloned.1.call-done = f32[1024,128]{0,1:T(8,128)} async-done(((f32[1024,128]{0,1:T(8,128)}), f32[1024,128]{0,1:T(8,128)}) %all-reduce.3.cloned.1.call-update) | async-done | bytes 524304
  807.0 0.9 constant_dynamic-slice_fusion
  (91 shorter events, 6.8 us)
Async XLA Ops:
  7.2 58.7 %copy-start = (bf16[128,1024]{1,0:T(8,128)(2,1)S(1)}, bf16[128,1024]{1,0:T(8,128)(2,1)}, u32[]{:S(2)}) copy-start(bf16[128,1024]{1,0:T(8,128)(2,1)} %param.6) | copy-start | bytes 786436
  7.2 25.2 %copy-start.5 = (bf16[128,2048]{1,0:T(8,128)(2,1)S(1)}, bf16[128,2048]{1,0:T(8,128)(2,1)}, u32[]{:S(2)}) copy-start(bf16[128,2048]{1,0:T(8,128)(2,1)} %param.11) | copy-start | bytes 1572868
  8.3 24.5 %copy-start.4 = (bf16[128,2048]{1,0:T(8,128)(2,1)S(1)}, bf16[128,2048]{1,0:T(8,128)(2,1)}, u32[]{:S(2)}) copy-start(bf16[128,2048]{1,0:T(8,128)(2,1)} %param.7) | copy-start | bytes 1572868
  8.3 28.3 %collective-permute-start = (f32[32]{0:T(128)S(1)}, f32[32]{0:T(128)S(1)}, u32[]{:S(2)}, u32[]{:S(2)}) collective-permute-start(f32[32]{0:T(128)S(1)} %slice_bitcast_fusion), channel_id=1, source_target_pairs={{1,0},{2,1},{3,2},{4,3},{5,4},{6,5},{7,6},{8,7},{9,8},{10,9},{11,1... | collective-permute-start | bytes 392 | tf_op jit(solution)/shard_map/ppermute | solution.py:14
  11.6 28.2 %collective-permute-start.17 = (f32[32]{0:T(128)S(1)}, f32[32]{0:T(128)S(1)}, u32[]{:S(2)}, u32[]{:S(2)}) collective-permute-start(f32[32]{0:T(128)S(1)} %slice_bitcast_fusion), channel_id=1, source_target_pairs={{0,1},{1,2},{2,3},{3,4},{4,5},{5,6},{6,7},{7,8},{8,9},{9,10},{10,1... | collective-permute-start | bytes 392 | tf_op jit(solution)/shard_map/ppermute | solution.py:14
  15.0 50.8 %all-to-all-start = ((bf16[256,4,128]{2,1,0:T(4,128)(2,1)}), bf16[256,4,128]{2,1,0:T(4,128)(2,1)S(1)}, u32[]{:S(2)}, u32[]{:S(2)}) async-start(bf16[256,4,128]{2,1,0:T(4,128)(2,1)} %stack.2), calls=%async_computation | async-start | bytes 524288 | tf_op jit(solution)/shard_map/all_to_all | solution.py:77
  32.2 774.8 %all-reduce.3.cloned.1.call-start = ((), (), s32[]{:S(2)}) async-start(), calls=%async_computation.1 | async-start | bytes 1048576
  32.3 1.8 copy-start.9
  33.0 1.2 copy-start.6
  36.6 5.2 collective-permute-start.1
  39.8 5.8 collective-permute-start.18
  41.8 5.9 collective-permute-start.2
  45.6 6.3 collective-permute-start.19
  47.7 7.6 collective-permute-start.3
  51.9 5.4 collective-permute-start.20
  55.4 13.7 %collective-permute-start.4 = (f32[32]{0:T(128)S(1)}, f32[32]{0:T(128)S(1)}, u32[]{:S(2)}, u32[]{:S(2)}) collective-permute-start(f32[32]{0:T(128)S(1)} %get-tuple-element.188), channel_id=1, source_target_pairs={{8,0},{9,1},{10,2},{11,3},{12,4},{13,5},{14,6},{15,7},{16,8},{17,9... | collective-permute-start | bytes 392 | tf_op jit(solution)/shard_map/ppermute | solution.py:14
  57.4 16.4 %collective-permute-start.21 = (f32[32]{0:T(128)S(1)}, f32[32]{0:T(128)S(1)}, u32[]{:S(2)}, u32[]{:S(2)}) collective-permute-start(f32[32]{0:T(128)S(1)} %get-tuple-element.176), channel_id=1, source_target_pairs={{0,8},{1,9},{2,10},{3,11},{4,12},{5,13},{6,14},{7,15},{8,16},{9,17... | collective-permute-start | bytes 392 | tf_op jit(solution)/shard_map/ppermute | solution.py:14
  65.9 1.3 copy-start.2
  67.1 19.8 %collective-permute-start.8 = (f32[32,64,64]{2,1,0:T(8,128)S(1)}, f32[32,64,64]{2,1,0:T(8,128)S(1)}, u32[]{:S(2)}, u32[]{:S(2)}) collective-permute-start(f32[32,64,64]{2,1,0:T(8,128)S(1)} %fusion.19), channel_id=1, source_target_pairs={{1,0},{2,1},{3,2},{4,3},{5,4},{6,5},{7,6},{8,7},{9,8},{10,9},{11,1... | collective-permute-start | bytes 1572872 | tf_op jit(solution)/shard_map/ppermute | solution.py:14
  69.1 22.6 %collective-permute-start.5 = (f32[32]{0:T(128)S(1)}, f32[32]{0:T(128)S(1)}, u32[]{:S(2)}, u32[]{:S(2)}) collective-permute-start(f32[32]{0:T(128)S(1)} %get-tuple-element.186), channel_id=1, source_target_pairs={{16,0},{17,1},{18,2},{19,3},{20,4},{21,5},{22,6},{23,7},{24,8},{25... | collective-permute-start | bytes 392 | tf_op jit(solution)/shard_map/ppermute | solution.py:14
  71.4 34.2 %collective-permute-start.25 = (f32[32,64,64]{2,1,0:T(8,128)S(1)}, f32[32,64,64]{2,1,0:T(8,128)S(1)}, u32[]{:S(2)}, u32[]{:S(2)}) collective-permute-start(f32[32,64,64]{2,1,0:T(8,128)S(1)} %fusion.22), channel_id=1, source_target_pairs={{0,1},{1,2},{2,3},{3,4},{4,5},{5,6},{6,7},{7,8},{8,9},{9,10},{10,1... | collective-permute-start | bytes 1572872 | tf_op jit(solution)/shard_map/ppermute | solution.py:14
  73.8 19.2 %collective-permute-start.22 = (f32[32]{0:T(128)S(1)}, f32[32]{0:T(128)S(1)}, u32[]{:S(2)}, u32[]{:S(2)}) collective-permute-start(f32[32]{0:T(128)S(1)} %get-tuple-element.174), channel_id=1, source_target_pairs={{0,16},{1,17},{2,18},{3,19},{4,20},{5,21},{6,22},{7,23},{8,24},{9,... | collective-permute-start | bytes 392 | tf_op jit(solution)/shard_map/ppermute | solution.py:14
  87.0 29.1 %collective-permute-start.9 = (f32[32,64,64]{2,1,0:T(8,128)S(1)}, f32[32,64,64]{2,1,0:T(8,128)S(1)}, u32[]{:S(2)}, u32[]{:S(2)}) collective-permute-start(f32[32,64,64]{2,1,0:T(8,128)S(1)} %collective-permute-done.8), channel_id=1, source_target_pairs={{1,0},{2,1},{3,2},{4,3},{5,4},{6,5},{7,6},{8,7},{9,8},{10,9},{11,1... | collective-permute-start | bytes 1572872 | tf_op jit(solution)/shard_map/ppermute | solution.py:14
  91.7 23.0 %collective-permute-start.6 = (f32[32]{0:T(128)S(1)}, f32[32]{0:T(128)S(1)}, u32[]{:S(2)}, u32[]{:S(2)}) collective-permute-start(f32[32]{0:T(128)S(1)} %get-tuple-element.184), channel_id=1, source_target_pairs={{32,0},{33,1},{34,2},{35,3},{36,4},{37,5},{38,6},{39,7},{40,8},{41... | collective-permute-start | bytes 392 | tf_op jit(solution)/shard_map/ppermute | solution.py:14
  93.0 33.4 %collective-permute-start.23 = (f32[32]{0:T(128)S(1)}, f32[32]{0:T(128)S(1)}, u32[]{:S(2)}, u32[]{:S(2)}) collective-permute-start(f32[32]{0:T(128)S(1)} %get-tuple-element.172), channel_id=1, source_target_pairs={{0,32},{1,33},{2,34},{3,35},{4,36},{5,37},{6,38},{7,39},{8,40},{9,... | collective-permute-start | bytes 392 | tf_op jit(solution)/shard_map/ppermute | solution.py:14
  105.6 18.7 %collective-permute-start.26 = (f32[32,64,64]{2,1,0:T(8,128)S(1)}, f32[32,64,64]{2,1,0:T(8,128)S(1)}, u32[]{:S(2)}, u32[]{:S(2)}) collective-permute-start(f32[32,64,64]{2,1,0:T(8,128)S(1)} %collective-permute-done.25), channel_id=1, source_target_pairs={{0,1},{1,2},{2,3},{3,4},{4,5},{5,6},{6,7},{7,8},{8,9},{9,10},{10,1... | collective-permute-start | bytes 1572872 | tf_op jit(solution)/shard_map/ppermute | solution.py:14
  114.7 75.8 %collective-permute-start.7 = (f32[32]{0:T(128)S(1)}, f32[32]{0:T(128)S(1)}, u32[]{:S(2)}, u32[]{:S(2)}) collective-permute-start(f32[32]{0:T(128)S(1)} %get-tuple-element.182), channel_id=1, source_target_pairs={{64,0},{65,1},{66,2},{67,3},{68,4},{69,5},{70,6},{71,7},{72,8},{73... | collective-permute-start | bytes 392 | tf_op jit(solution)/shard_map/ppermute | solution.py:14
  116.2 28.0 %collective-permute-start.10 = (f32[32,64,64]{2,1,0:T(8,128)S(1)}, f32[32,64,64]{2,1,0:T(8,128)S(1)}, u32[]{:S(2)}, u32[]{:S(2)}) collective-permute-start(f32[32,64,64]{2,1,0:T(8,128)S(1)} %multiply_add_fusion.14), channel_id=1, source_target_pairs={{2,0},{3,1},{4,2},{5,3},{6,4},{7,5},{8,6},{9,7},{10,8},{11,9},{12,... | collective-permute-start | bytes 1572872 | tf_op jit(solution)/shard_map/ppermute | solution.py:14
  124.5 63.8 %collective-permute-start.27 = (f32[32,64,64]{2,1,0:T(8,128)S(1)}, f32[32,64,64]{2,1,0:T(8,128)S(1)}, u32[]{:S(2)}, u32[]{:S(2)}) collective-permute-start(f32[32,64,64]{2,1,0:T(8,128)S(1)} %multiply_add_fusion.6), channel_id=1, source_target_pairs={{0,2},{1,3},{2,4},{3,5},{4,6},{5,7},{6,8},{7,9},{8,10},{9,11},{10,... | collective-permute-start | bytes 1572872 | tf_op jit(solution)/shard_map/ppermute | solution.py:14
  126.5 94.4 %collective-permute-start.24 = (f32[32]{0:T(128)S(1)}, f32[32]{0:T(128)S(1)}, u32[]{:S(2)}, u32[]{:S(2)}) collective-permute-start(f32[32]{0:T(128)S(1)} %get-tuple-element.170), channel_id=1, source_target_pairs={{0,64},{1,65},{2,66},{3,67},{4,68},{5,69},{6,70},{7,71},{8,72},{9,... | collective-permute-start | bytes 392 | tf_op jit(solution)/shard_map/ppermute | solution.py:14
  144.3 46.2 %collective-permute-start.11 = (f32[32,64,64]{2,1,0:T(8,128)S(1)}, f32[32,64,64]{2,1,0:T(8,128)S(1)}, u32[]{:S(2)}, u32[]{:S(2)}) collective-permute-start(f32[32,64,64]{2,1,0:T(8,128)S(1)} %multiply_add_fusion.13), channel_id=1, source_target_pairs={{4,0},{5,1},{6,2},{7,3},{8,4},{9,5},{10,6},{11,7},{12,8},{13,9},{1... | collective-permute-start | bytes 1572872 | tf_op jit(solution)/shard_map/ppermute | solution.py:14
  188.5 30.8 %collective-permute-start.28 = (f32[32,64,64]{2,1,0:T(8,128)S(1)}, f32[32,64,64]{2,1,0:T(8,128)S(1)}, u32[]{:S(2)}, u32[]{:S(2)}) collective-permute-start(f32[32,64,64]{2,1,0:T(8,128)S(1)} %multiply_add_fusion.5), channel_id=1, source_target_pairs={{0,4},{1,5},{2,6},{3,7},{4,8},{5,9},{6,10},{7,11},{8,12},{9,13},{1... | collective-permute-start | bytes 1572872 | tf_op jit(solution)/shard_map/ppermute | solution.py:14
  190.5 282.6 %copy-start.11 = (f32[32]{0:T(128)}, f32[32]{0:T(128)S(1)}, u32[]{:S(2)}) copy-start(f32[32]{0:T(128)S(1)} %add_exponential_fusion.1) | copy-start | bytes 388
  190.7 30.2 %collective-permute-start.12 = (f32[32,64,64]{2,1,0:T(8,128)S(1)}, f32[32,64,64]{2,1,0:T(8,128)S(1)}, u32[]{:S(2)}, u32[]{:S(2)}) collective-permute-start(f32[32,64,64]{2,1,0:T(8,128)S(1)} %multiply_add_fusion.12), channel_id=1, source_target_pairs={{8,0},{9,1},{10,2},{11,3},{12,4},{13,5},{14,6},{15,7},{16,8},{17,9... | collective-permute-start | bytes 1572872 | tf_op jit(solution)/shard_map/ppermute | solution.py:14
  219.5 24.6 %collective-permute-start.29 = (f32[32,64,64]{2,1,0:T(8,128)S(1)}, f32[32,64,64]{2,1,0:T(8,128)S(1)}, u32[]{:S(2)}, u32[]{:S(2)}) collective-permute-start(f32[32,64,64]{2,1,0:T(8,128)S(1)} %multiply_add_fusion.4), channel_id=1, source_target_pairs={{0,8},{1,9},{2,10},{3,11},{4,12},{5,13},{6,14},{7,15},{8,16},{9,17... | collective-permute-start | bytes 1572872 | tf_op jit(solution)/shard_map/ppermute | solution.py:14
  221.1 26.6 %collective-permute-start.13 = (f32[32,64,64]{2,1,0:T(8,128)S(1)}, f32[32,64,64]{2,1,0:T(8,128)S(1)}, u32[]{:S(2)}, u32[]{:S(2)}) collective-permute-start(f32[32,64,64]{2,1,0:T(8,128)S(1)} %multiply_add_fusion.11), channel_id=1, source_target_pairs={{16,0},{17,1},{18,2},{19,3},{20,4},{21,5},{22,6},{23,7},{24,8},{25... | collective-permute-start | bytes 1572872 | tf_op jit(solution)/shard_map/ppermute | solution.py:14
  244.3 15.3 %collective-permute-start.30 = (f32[32,64,64]{2,1,0:T(8,128)S(1)}, f32[32,64,64]{2,1,0:T(8,128)S(1)}, u32[]{:S(2)}, u32[]{:S(2)}) collective-permute-start(f32[32,64,64]{2,1,0:T(8,128)S(1)} %multiply_add_fusion.3), channel_id=1, source_target_pairs={{0,16},{1,17},{2,18},{3,19},{4,20},{5,21},{6,22},{7,23},{8,24},{9,... | collective-permute-start | bytes 1572872 | tf_op jit(solution)/shard_map/ppermute | solution.py:14
  247.8 87.1 %collective-permute-start.14 = (f32[32,64,64]{2,1,0:T(8,128)S(1)}, f32[32,64,64]{2,1,0:T(8,128)S(1)}, u32[]{:S(2)}, u32[]{:S(2)}) collective-permute-start(f32[32,64,64]{2,1,0:T(8,128)S(1)} %multiply_add_fusion.10), channel_id=1, source_target_pairs={{32,0},{33,1},{34,2},{35,3},{36,4},{37,5},{38,6},{39,7},{40,8},{41... | collective-permute-start | bytes 1572872 | tf_op jit(solution)/shard_map/ppermute | solution.py:14
  259.6 61.3 %copy-start.10 = (pred[128,128]{0,1:T(8,128)(4,1)S(1)}, pred[128,128]{0,1:T(8,128)(4,1)}, u32[]{:S(2)}) copy-start(pred[128,128]{0,1:T(8,128)(4,1)} %copy-done.9) | copy-start | bytes 49156
  259.7 107.9 %collective-permute-start.31 = (f32[32,64,64]{2,1,0:T(8,128)S(1)}, f32[32,64,64]{2,1,0:T(8,128)S(1)}, u32[]{:S(2)}, u32[]{:S(2)}) collective-permute-start(f32[32,64,64]{2,1,0:T(8,128)S(1)} %multiply_add_fusion.2), channel_id=1, source_target_pairs={{0,32},{1,33},{2,34},{3,35},{4,36},{5,37},{6,38},{7,39},{8,40},{9,... | collective-permute-start | bytes 1572872 | tf_op jit(solution)/shard_map/ppermute | solution.py:14
  335.1 85.0 %collective-permute-start.15 = (f32[32,64,64]{2,1,0:T(8,128)S(1)}, f32[32,64,64]{2,1,0:T(8,128)S(1)}, u32[]{:S(2)}, u32[]{:S(2)}) collective-permute-start(f32[32,64,64]{2,1,0:T(8,128)S(1)} %multiply_add_fusion.9), channel_id=1, source_target_pairs={{64,0},{65,1},{66,2},{67,3},{68,4},{69,5},{70,6},{71,7},{72,8},{73... | collective-permute-start | bytes 1572872 | tf_op jit(solution)/shard_map/ppermute | solution.py:14
  367.8 74.9 %collective-permute-start.32 = (f32[32,64,64]{2,1,0:T(8,128)S(1)}, f32[32,64,64]{2,1,0:T(8,128)S(1)}, u32[]{:S(2)}, u32[]{:S(2)}) collective-permute-start(f32[32,64,64]{2,1,0:T(8,128)S(1)} %multiply_add_fusion.1), channel_id=1, source_target_pairs={{0,64},{1,65},{2,66},{3,67},{4,68},{5,69},{6,70},{7,71},{8,72},{9,... | collective-permute-start | bytes 1572872 | tf_op jit(solution)/shard_map/ppermute | solution.py:14
  420.3 52.8 %collective-permute-start.16 = (f32[32,64,64]{2,1,0:T(8,128)S(1)}, f32[32,64,64]{2,1,0:T(8,128)S(1)}, u32[]{:S(2)}, u32[]{:S(2)}) collective-permute-start(f32[32,64,64]{2,1,0:T(8,128)S(1)} %multiply_add_fusion.8), channel_id=1, source_target_pairs={{128,0},{129,1},{130,2},{131,3},{132,4},{133,5},{134,6},{135,7},{1... | collective-permute-start | bytes 1572872 | tf_op jit(solution)/shard_map/ppermute | solution.py:14
  442.6 30.5 %copy-start.7 = (f32[128,32]{0,1:T(8,128)S(1)}, f32[128,32]{0,1:T(8,128)}, u32[]{:S(2)}) copy-start(f32[128,32]{0,1:T(8,128)} %param.8) | copy-start | bytes 49156
  442.8 33.4 %collective-permute-start.33 = (f32[32,64,64]{2,1,0:T(8,128)S(1)}, f32[32,64,64]{2,1,0:T(8,128)S(1)}, u32[]{:S(2)}, u32[]{:S(2)}) collective-permute-start(f32[32,64,64]{2,1,0:T(8,128)S(1)} %multiply_add_fusion), channel_id=1, source_target_pairs={{0,128},{1,129},{2,130},{3,131},{4,132},{5,133},{6,134},{7,135},{8... | collective-permute-start | bytes 1572872 | tf_op jit(solution)/shard_map/ppermute | solution.py:14
  454.7 21.5 %copy-start.1 = (f32[128,2048]{0,1:T(8,128)S(1)}, f32[128,2048]{0,1:T(8,128)}, u32[]{:S(2)}) copy-start(f32[128,2048]{0,1:T(8,128)} %bitcast_multiply_fusion.1) | copy-start | bytes 3145732
  478.2 1.1 copy-start.8
  478.2 1.1 copy-start.12
  481.5 1.3 copy-start.3
Sparse Core Ops, SparseCore 0:
  479.4 327.5 all-reduce.2
